TPU v7x, 32 devices: a whole 2x2x4 slice. The times are simulated.
32 devices in a mesh: seq: 16 (over z, y, core), head: 2 (over x).
Axes of the slice: x: 2, y: 2, z: 4, core: 2. Of those that a mesh axis runs over, the one named last changes fastest.
Arguments:
- queries: bfloat16 [6144, 768], P('seq', 'head'), as said below
- keys: bfloat16 [6144, 768], P('seq', 'head'), as said below
- values: bfloat16 [6144, 768], P('seq', 'head'), may hold values from -6 to 6
- image_tiles: int32 [5], replicated, may hold values from 1 to 21, 48 in all
Outputs:
- attended: bfloat16 [6144, 768], P(('seq', 'head'))
Inputs may be any that keep to these rules, and one draw needn't show every extreme that they name: `image_tiles`: the 5 images fill all 48 tiles in order; the longest holds exactly 21 tiles. `queries`: entries lie within -6 and 6. `keys`: entries lie within -6 and 6.
All inputs are finite; a program needn't handle non-finite values.
Results may differ from a plain program's by a relative error of at most 0.007.
Values may be sent and summed in bfloat16 or wider, within the bound.
No kernel may reach another device: no remote copies, remote signals or barrier semaphores. Data moves between devices by JAX's collectives and lax.ppermute only.
A program may use at most 64 MiB of HBM per device.

v0:
```python
import functools
import math

import jax
import jax.numpy as jnp
from jax import lax
from jax.experimental import pallas as pl
from jax.experimental.pallas import tpu as pltpu
from jax.sharding import PartitionSpec as P

HEAD_DIM = 128
TILE = 128
MOST_TILES = 21

LOWEST = -1e30
SCALE2 = math.log2(math.e) / math.sqrt(HEAD_DIM)
COST = 6

VMEM = pl.BlockSpec(memory_space=pltpu.VMEM)
SMEM = pl.BlockSpec(memory_space=pltpu.SMEM)
HBM = pl.BlockSpec(memory_space=pl.ANY)


def params():
    return pltpu.CompilerParams(vmem_limit_bytes=32 * 1024 * 1024)


def head_columns(h):
    return slice(h * HEAD_DIM, (h + 1) * HEAD_DIM)


def tile_rows(t):
    return slice(t * TILE, (t + 1) * TILE)


def image_bounds(tiles_ref, tile):
    first = jnp.int32(0)
    start, end = jnp.int32(0), jnp.int32(0)
    for i in range(tiles_ref.shape[0]):
        after = first + tiles_ref[i]
        inside = (tile >= first) & (tile < after)
        start = jnp.where(inside, first, start)
        end = jnp.where(inside, after, end)
        first = after
    return start, end


def chip_spans(tiles_ref, chip_tiles):
    first = jnp.int32(0)
    even, odd, four = jnp.int32(0), jnp.int32(0), jnp.int32(0)
    for i in range(tiles_ref.shape[0]):
        after = first + tiles_ref[i]
        low, high = first // chip_tiles, (after - 1) // chip_tiles
        parity = low % 2
        even = jnp.where(high - (low + parity) >= 3, 1, even)
        odd = jnp.where(high - (low + 1 - parity) >= 3, 1, odd)
        four = jnp.where(high - low >= 4, 1, four)
        first = after
    return jnp.where(odd + four == 0, 0, jnp.where(even + four == 0, 1, 2)).astype(jnp.int32)


def meta_kernel(halves, tiles_ref, bounds_ref, spans_ref):
    tiles = bounds_ref.shape[1] // TILE
    me = lax.axis_index("seq")
    bounds_ref[...] = jnp.zeros(bounds_ref.shape, jnp.int32)
    for half, owner in enumerate(halves(me)):
        for t in range(tiles):
            start, end = image_bounds(tiles_ref, owner * tiles + t)
            bounds_ref[2 * half : 2 * half + 1, tile_rows(t)] = jnp.full((1, TILE), start, jnp.int32)
            bounds_ref[2 * half + 1 : 2 * half + 2, tile_rows(t)] = jnp.full((1, TILE), end, jnp.int32)
    spans_ref[0] = chip_spans(tiles_ref, 2 * tiles)


def meta(halves, image_tiles, rows):
    bounds, spans = pl.pallas_call(
        functools.partial(meta_kernel, halves),
        out_shape=[jax.ShapeDtypeStruct((8, rows), jnp.int32), jax.ShapeDtypeStruct((1,), jnp.int32)],
        in_specs=[SMEM],
        out_specs=[VMEM, SMEM],
        compiler_params=params(),
        cost_estimate=pl.CostEstimate(flops=COST * 2**29, bytes_accessed=0, transcendentals=0),
        name="meta",
    )(image_tiles)
    return bounds, spans[0]


def pack_kernel(k_ref, v_ref, out_ref, held, sems):
    rows, columns = k_ref.shape
    tiles = rows // TILE
    copies = []
    for t in range(tiles):
        copies.append(pltpu.make_async_copy(v_ref.at[tile_rows(t)], held.at[tile_rows(t)], sems.at[2 * t]))
        copies.append(pltpu.make_async_copy(k_ref.at[tile_rows(t)], out_ref.at[tile_rows(2 * t)], sems.at[2 * t + 1]))
    for copy in copies:
        copy.start()
    for t in range(tiles):
        copies[2 * t].wait()
        for h in range(columns // HEAD_DIM):
            out_ref[tile_rows(2 * t + 1), head_columns(h)] = held[tile_rows(t), head_columns(h)].T
    for copy in copies[1::2]:
        copy.wait()


def pack(keys, values):
    rows, columns = keys.shape
    return pl.pallas_call(
        pack_kernel,
        out_shape=jax.ShapeDtypeStruct((2 * rows, columns), keys.dtype),
        in_specs=[HBM, HBM],
        out_specs=VMEM,
        scratch_shapes=[pltpu.VMEM(values.shape, values.dtype), pltpu.SemaphoreType.DMA((2 * rows // TILE,))],
        name="pack",
    )(keys, values)


def corner_kernel(a1_ref, b1_ref, out_ref):
    me = lax.axis_index("seq")
    rows = pl.ds(pl.multiple_of((me % 2) * 2 * TILE, 2 * TILE), out_ref.shape[0])

    @pl.when((me // 2) % 2 == 0)
    def _():
        out_ref[...] = a1_ref[rows]

    @pl.when((me // 2) % 2 == 1)
    def _():
        out_ref[...] = b1_ref[rows]


def corner_of(a1, b1):
    return pl.pallas_call(
        corner_kernel,
        out_shape=jax.ShapeDtypeStruct((a1.shape[0] - 2 * TILE, a1.shape[1]), a1.dtype),
        in_specs=[VMEM, VMEM],
        out_specs=VMEM,
        compiler_params=params(),
        name="corner",
    )(a1, b1)


def attend_kernel(which, places, arrays, fresh, bounds_ref, *refs):
    halves = len(which)
    q_refs, refs = refs[:halves], refs[halves:]
    array_refs, refs = refs[: len(arrays)], refs[len(arrays) :]
    old_refs, refs = (None, refs) if fresh else (refs[:halves], refs[halves:])
    new_refs, (held_q, held, state) = refs[:halves], refs[halves:]
    rows, columns = q_refs[0].shape
    tiles = rows // TILE
    count = held.shape[1] // 2 // TILE
    heads = columns // HEAD_DIM
    me = lax.axis_index("seq")

    for half in range(halves):
        held_q[half] = q_refs[half][...]
        if fresh:
            state[half, :columns] = jnp.zeros((columns, rows), jnp.float32)
            state[half, columns : columns + heads] = jnp.full((heads, rows), LOWEST, jnp.float32)
            state[half, columns + heads :] = jnp.zeros((state.shape[1] - columns - heads, rows), jnp.float32)
        else:
            state[half] = old_refs[half][...]
    for slot, (array, shift) in enumerate(arrays):
        size = array_refs[array].shape[0]
        if size < held.shape[1]:
            held[slot] = jnp.zeros(held.shape[1:], held.dtype)
        at = 0 if shift is None else pl.multiple_of(shift(me), 2 * TILE)
        held[slot, pl.ds(at, size)] = array_refs[array][...]
    begins = [bounds_ref[2 * w, 0] for w in which]
    stops = [bounds_ref[2 * w + 1, rows - 1] for w in which]

    def chosen(at, options):
        return functools.reduce(lambda x, i: jnp.where(at == i, options[i], x), range(1, len(options)), options[0])

    def fold(half, slot, first):
        low = bounds_ref[pl.ds(2 * (half + which[0]), 1), :]
        high = bounds_ref[pl.ds(2 * (half + which[0]) + 1, 1), :]
        off = [
            jnp.where((first + j >= low) & (first + j < high), 0.0, -LOWEST).astype(jnp.float32)
            for j in range(count)
        ]
        for h in range(heads):
            own = head_columns(h)
            scores = lax.dot_general(
                jnp.concatenate([held[slot, tile_rows(2 * j), own] for j in range(count)], axis=0),
                held_q[half, :, own],
                (((1,), (1,)), ((), ())),
                preferred_element_type=jnp.float32,
            )
            max_at, total_at = pl.ds(columns + h, 1), pl.ds(columns + heads + h, 1)
            factors, rounded, totals, maxima = [], [], [], []
            for t in range(tiles):
                lanes = tile_rows(t)
                parts = [scores[tile_rows(j), lanes] for j in range(count)]
                old_max = state[half, max_at, lanes]
                new_max = old_max
                for j in range(count):
                    new_max = jnp.maximum(new_max, jnp.max(parts[j], axis=0, keepdims=True) - off[j][:, lanes])
                scaled = new_max * SCALE2
                weights = [jnp.exp2(parts[j] * SCALE2 - (scaled + off[j][:, lanes])) for j in range(count)]
                factors.append(jnp.exp2((old_max - new_max) * SCALE2))
                totals.append(jnp.sum(functools.reduce(jnp.add, weights), axis=0, keepdims=True))
                maxima.append(new_max)
                rounded.append(jnp.concatenate([w.astype(jnp.bfloat16) for w in weights], axis=0))
            factor = jnp.concatenate(factors, axis=1)
            update = jnp.dot(
                jnp.concatenate([held[slot, tile_rows(2 * j + 1), own] for j in range(count)], axis=1),
                jnp.concatenate(rounded, axis=1),
                preferred_element_type=jnp.float32,
            )
            state[half, own] = state[half, own] * factor + update
            state[half, max_at] = jnp.concatenate(maxima, axis=1)
            state[half, total_at] = state[half, total_at] * factor + jnp.concatenate(totals, axis=1)

    @pl.loop(0, halves * len(places))
    def _(unit):
        half, slot = unit // len(places), unit % len(places)
        first = chosen(slot, [place(me) for place in places])

        @pl.when((first < chosen(half, stops)) & (first + count > chosen(half, begins)))
        def _():
            fold(half, slot, first)

    for half in range(halves):
        new_refs[half][...] = state[half]


def attend(bounds, queries, blocks, places, states, which=None, shifts=None):
    which = list(range(len(queries))) if which is None else which
    queries, states = [queries[w] for w in which], [states[w] for w in which] if states else []
    halves = len(which)
    rows, columns = queries[0].shape
    depth = blocks[0].shape[0]
    heads = columns // HEAD_DIM
    shape = jax.ShapeDtypeStruct((columns + -(-2 * heads // 8) * 8, rows), jnp.float32)
    arrays = list(enumerate(shifts or [None] * len(blocks)))
    pairs = halves * (rows // TILE) * heads * len(blocks) * (depth // 2 // TILE)
    return pl.pallas_call(
        functools.partial(attend_kernel, which, places, arrays, not states),
        out_shape=[shape] * halves,
        in_specs=[VMEM] * (1 + halves + len(blocks) + len(states)),
        out_specs=[VMEM] * halves,
        scratch_shapes=[
            pltpu.VMEM((halves, rows, columns), queries[0].dtype),
            pltpu.VMEM((len(blocks), depth, columns), blocks[0].dtype),
            pltpu.VMEM((halves,) + shape.shape, jnp.float32),
        ],
        compiler_params=params(),
        cost_estimate=pl.CostEstimate(
            flops=COST * pairs * 4 * TILE * TILE * HEAD_DIM,
            bytes_accessed=2 * len(blocks) * depth * columns + 4 * halves * rows * columns,
            transcendentals=pairs * TILE * TILE,
        ),
        name="attend",
    )(bounds, *queries, *blocks, *states)


def merged(states, columns):
    heads = columns // HEAD_DIM
    for h in range(heads):
        maxima = [ref[columns + h : columns + h + 1] for ref in states]
        totals = [ref[columns + heads + h : columns + heads + h + 1] for ref in states]
        largest = functools.reduce(jnp.maximum, maxima)
        factors = [jnp.exp2((m - largest) * SCALE2) for m in maxima]
        total = functools.reduce(jnp.add, [f * t for f, t in zip(factors, totals)])
        parts = [ref[head_columns(h)] * (f / total) for ref, f in zip(states, factors)]
        yield head_columns(h), functools.reduce(jnp.add, parts).T


def finish_kernel(*refs):
    out_ref = refs[-1]
    for own, done in merged(refs[:-1], out_ref.shape[1]):
        out_ref[:, own] = done.astype(out_ref.dtype)


def finish(states, rows, columns):
    return pl.pallas_call(
        finish_kernel,
        out_shape=jax.ShapeDtypeStruct((rows, columns), jnp.bfloat16),
        in_specs=[VMEM] * len(states),
        out_specs=VMEM,
        compiler_params=params(),
        name="finish",
    )(*states)


def part_kernel(*refs):
    keep_ref, send_ref, held = refs[-3:]
    rows, columns = keep_ref.shape
    mine = lax.axis_index("head")
    for own, done in merged(refs[:-3], columns):
        held[:, own] = done.astype(held.dtype)
    send_ref[...] = held[pl.ds(pl.multiple_of((1 - mine) * rows, 16), rows), :]
    keep_ref[...] = held[pl.ds(pl.multiple_of(mine * rows, 16), rows), :]


def join_kernel(keep_ref, got_ref, out_ref):
    columns = keep_ref.shape[1]
    mine = lax.axis_index("head")
    out_ref[:, pl.ds(pl.multiple_of(mine * columns, TILE), columns)] = keep_ref[...]
    out_ref[:, pl.ds(pl.multiple_of((1 - mine) * columns, TILE), columns)] = got_ref[...]


def finish_in_two(states, rows, columns):
    part = jax.ShapeDtypeStruct((rows // 2, columns), jnp.bfloat16)
    keep, send = pl.pallas_call(
        part_kernel,
        out_shape=[part, part],
        in_specs=[VMEM] * len(states),
        out_specs=[VMEM, VMEM],
        scratch_shapes=[pltpu.VMEM((rows, columns), jnp.bfloat16)],
        compiler_params=params(),
        name="part",
    )(*states)
    got = lax.ppermute(send, "head", [(0, 1), (1, 0)])
    return pl.pallas_call(
        join_kernel,
        out_shape=jax.ShapeDtypeStruct((rows // 2, 2 * columns), jnp.bfloat16),
        in_specs=[VMEM, VMEM],
        out_specs=VMEM,
        compiler_params=params(),
        name="join",
    )(keep, got)


def chip_pairs(mesh):
    places = [tuple(getattr(d, "coords", ())) for d in mesh.devices[:, 0]]
    count = len(places)
    if count % 4 or not places[0] or mesh.shape["head"] != 2:
        return False
    cores = all(places[i] == places[i + 1] for i in range(0, count, 2))
    level = all(places[i][2] == places[i + 3][2] for i in range(0, count, 4))
    climb = all(places[i][2] != places[i + 4][2] for i in range(0, count - 4))
    return cores and level and climb


def paired_shards(owner_count, queries, keys, values, image_tiles):
    rows, columns = queries.shape
    tiles = rows // TILE

    def flip(s):
        return 1 - 2 * ((s // 2) % 2)

    def core(s):
        return s % 2

    def turn(s):
        return flip(s) * (1 - 2 * core(s))

    def moved(array, source, takes=lambda s: True):
        pairs = [(source(s), s) for s in range(owner_count) if takes(s) and 0 <= source(s) < owner_count]
        return lax.ppermute(array, "seq", pairs)

    across = lambda s: s + 2 * flip(s)
    along = lambda s: s + 4 * turn(s)
    against = lambda s: s - 4 * turn(s)
    sibling = lambda s: s + 1 - 2 * core(s)

    nobody = -owner_count
    OWN = lambda s: s * tiles
    Y1 = lambda s: across(s) * tiles
    A1 = lambda s: along(s) * tiles
    B1 = lambda s: against(s) * tiles
    YA = lambda s: (s + 2 * flip(s) - 4 * turn(s)) * tiles
    AY = lambda s: (s + 2 * flip(s) + 4 * turn(s)) * tiles
    AY_OR_AA = lambda s: jnp.where(core(s) == 0, s + 8 * turn(s), s + 2 * flip(s) + 4 * turn(s)) * tiles
    THIRD = lambda s: (s - 6 * flip(s)) * tiles
    AY_LEFT = lambda s: jnp.where(core(s) == 0, s + 6 * flip(s), nobody) * tiles
    has_corner = lambda s: (core(s) == 1) | ((s // 2) % 2 == 1)
    CORNER = lambda s: jnp.where(has_corner(s), s + 8 * (1 - 2 * core(s)), nobody) * tiles

    block = pack(keys, values)
    y1, a1, b1 = moved(block, across), moved(block, along), moved(block, against)
    bounds, spans = meta(lambda s: [s, sibling(s)], image_tiles, rows)
    both = (queries, moved(queries, sibling))
    fold = functools.partial(attend, bounds, both)
    states = fold([block], [OWN], [])
    ay = moved(jnp.where((spans == 0) | (core(lax.axis_index("seq")) == 1), y1, a1), along)
    ya = moved(a1, across)
    states = fold([y1, a1, b1], [Y1, A1, B1], states)

    def last(blocks, places, states, shifts=None):
        (theirs,) = fold(blocks, places, states, which=[1], shifts=shifts)
        got = moved(theirs, sibling)
        (mine,) = fold(blocks, places, states, which=[0], shifts=shifts)
        return finish_in_two([mine, got], rows, columns)

    def near(y1, a1, b1, ya, ay, states):
        return last([ya, ay], [YA, AY], states)

    def third_of(ay):
        return moved(ay, lambda s: along(s) if core(s) else across(s))

    def odd(y1, a1, b1, ya, ay, states):
        third = third_of(ay)
        states = fold([ya, ay], [YA, AY_OR_AA], states)
        return last([third], [THIRD], states)

    def every_way(y1, a1, b1, ya, ay, states):
        third = third_of(ay)
        left = moved(y1, along, lambda s: core(s) == 0)
        corner = moved(corner_of(a1, b1), lambda s: s + 4 * (1 - 2 * core(s)), has_corner)
        states = fold([ya, ay], [YA, AY_OR_AA], states)
        shifts = [None, None, lambda s: 2 * TILE * core(s)]
        return last([third, left, corner], [THIRD, AY_LEFT, CORNER], states, shifts)

    return lax.switch(spans, [near, odd, every_way], y1, a1, b1, ya, ay, states)


def ring_shards(owner_count, queries, keys, values, image_tiles):
    rows, columns = queries.shape
    tiles = rows // TILE
    reach = min(owner_count - 1, -(-(MOST_TILES - 1) // tiles))
    block = pack(keys, values)
    bounds, _ = meta(lambda s: [s], image_tiles, rows)
    fold = functools.partial(attend, bounds, (queries,))
    up = [(i, i + 1) for i in range(owner_count - 1)]
    down = [(i + 1, i) for i in range(owner_count - 1)]
    below = above = block
    states = []
    held, places = [block], [lambda s: s * tiles]
    for k in range(1, reach + 1):
        below = lax.ppermute(below, "seq", up)
        above = lax.ppermute(above, "seq", down)
        states = fold(held, places, states)
        held, places = [below, above], [lambda s, k=k: (s - k) * tiles, lambda s, k=k: (s + k) * tiles]
    attended = finish(fold(held, places, states), rows, columns)
    return lax.all_to_all(attended, "head", split_axis=0, concat_axis=1, tiled=True)


def solution(mesh):
    owner_count = mesh.shape["seq"]
    plan = paired_shards if chip_pairs(mesh) else ring_shards
    placed = (P("seq", "head"), P("seq", "head"), P("seq", "head"), P())
    return jax.shard_map(
        functools.partial(plan, owner_count),
        mesh=mesh,
        in_specs=placed,
        out_specs=P(("seq", "head"), None),
        check_vma=False,
    )
```

profile of v0, /device:TPU:0, one launch (start us, length us, event | category | flops | bytes accessed | tf_op | source)
XLA Modules:
  0.0 47.7 jit_solution(4692662692846695738)
XLA Ops:
  0.0 0.0 copy-start.3
  0.0 0.0 copy-start.1
  0.0 2.1 %pack.1.refs_2_ = bf16[768,384]{1,0:T(8,128)(2,1)} custom-call(bf16[384,384]{1,0:T(8,128)(2,1)} %k_ref.1, bf16[384,384]{1,0:T(8,128)(2,1)} %v_ref.1), custom_call_target="tpu_custom_call" | custom-call | tf_op jit(solution)/shard_map/pack/pallas_call | solution.py:106
  2.1 0.0 copy-start
  2.1 3.0 %collective-permute-start.12 = (bf16[768,384]{1,0:T(8,128)(2,1)}, bf16[768,384]{1,0:T(8,128)(2,1)S(1)}, u32[]{:S(2)}, u32[]{:S(2)}) collective-permute-start(bf16[768,384]{1,0:T(8,128)(2,1)} %pack.1.refs_2_), channel_id=1, source_target_pairs={{4,0},{6,2},{0,4},{2,6},{12,8},{14,10},{8,12},{10,14},{20,16},{22,... | collective-permute-start | bytes 1769480 | tf_op jit(solution)/shard_map/ppermute | solution.py:349
  5.1 1.3 %collective-permute-start.10 = (bf16[768,384]{1,0:T(8,128)(2,1)}, bf16[768,384]{1,0:T(8,128)(2,1)S(1)}, u32[]{:S(2)}, u32[]{:S(2)}) collective-permute-start(bf16[768,384]{1,0:T(8,128)(2,1)} %pack.1.refs_2_), channel_id=1, source_target_pairs={{8,0},{14,6},{16,8},{2,10},{4,12},{22,14},{24,16},{10,18},{12,20},... | collective-permute-start | bytes 1769480 | tf_op jit(solution)/shard_map/ppermute | solution.py:349
  6.4 4.6 %collective-permute-start.15 = (bf16[768,384]{1,0:T(8,128)(2,1)}, bf16[768,384]{1,0:T(8,128)(2,1)S(1)}, u32[]{:S(2)}, u32[]{:S(2)}) collective-permute-start(bf16[768,384]{1,0:T(8,128)(2,1)} %pack.1.refs_2_), channel_id=1, source_target_pairs={{10,2},{12,4},{0,8},{18,10},{20,12},{6,14},{8,16},{26,18},{28,20},... | collective-permute-start | bytes 1769480 | tf_op jit(solution)/shard_map/ppermute | solution.py:349
  11.0 0.0 copy-done.3
  11.0 0.1 collective-permute-start.14
  11.1 0.0 copy-done.1
  11.1 1.2 %meta.1 = (s32[8,384]{1,0:T(8,128)S(1)}, s32[1]{0:T(128)}) custom-call(s32[5]{0:T(128)S(1)} %copy-done.1), custom_call_target="tpu_custom_call" | custom-call | flops 3221225472 | tf_op jit(solution)/shard_map/meta/pallas_call | solution.py:75
  13.6 0.0 collective-permute-done.14.refs_1_
  13.6 0.0 copy-start.5
  13.6 0.0 copy-done
  13.7 2.8 %attend.18 = (f32[392,384]{1,0:T(8,128)S(1)}, f32[392,384]{1,0:T(8,128)S(1)}) custom-call(s32[8,384]{1,0:T(8,128)S(1)} %get-tuple-element.98.bounds_ref, bf16[384,384]{1,0:T(8,128)(2,1)S(1)} %copy-done.3, bf16[384,384]{1,0:T(8,128)(2,1)S(1)} %collective-permute-done.14.refs_1_, bf16[768,384]{1,0:T(8,128)(2,1)S(1)} %copy-done), custom_call_target="tpu_custom_call" | custom-call | flops 2717908992 | bytes 1769472 | tf_op jit(solution)/shard_map/attend/pallas_call | solution.py:235
  16.4 0.0 copy-done.5
  16.4 0.0 copy-start.4
  16.4 2.2 %collective-permute-done.12.refs_2_ = bf16[768,384]{1,0:T(8,128)(2,1)S(1)} collective-permute-done((bf16[768,384]{1,0:T(8,128)(2,1)}, bf16[768,384]{1,0:T(8,128)(2,1)S(1)}, u32[]{:S(2)}, u32[]{:S(2)}) %collective-permute-start.12) | collective-permute-done | bytes 589856 | tf_op jit(solution)/shard_map/ppermute | solution.py:349
  18.7 0.0 copy-start.6
  18.7 2.9 %collective-permute-done.10.refs_3_ = bf16[768,384]{1,0:T(8,128)(2,1)S(1)} collective-permute-done((bf16[768,384]{1,0:T(8,128)(2,1)}, bf16[768,384]{1,0:T(8,128)(2,1)S(1)}, u32[]{:S(2)}, u32[]{:S(2)}) %collective-permute-start.10) | collective-permute-done | bytes 589856 | tf_op jit(solution)/shard_map/ppermute | solution.py:349
  21.5 0.1 broadcast_select_fusion
  21.6 1.3 %collective-permute-start.13 = (bf16[768,384]{1,0:T(8,128)(2,1)S(1)}, bf16[768,384]{1,0:T(8,128)(2,1)S(1)}, u32[]{:S(2)}, u32[]{:S(2)}) collective-permute-start(bf16[768,384]{1,0:T(8,128)(2,1)S(1)} %broadcast_select_fusion), channel_id=1, source_target_pairs={{8,0},{14,6},{16,8},{2,10},{4,12},{22,14},{24,16},{10,18},{12,20},... | collective-permute-start | bytes 1769480 | tf_op jit(solution)/shard_map/ppermute | solution.py:349
  22.9 4.2 %collective-permute-start.11 = (bf16[768,384]{1,0:T(8,128)(2,1)S(1)}, bf16[768,384]{1,0:T(8,128)(2,1)S(1)}, u32[]{:S(2)}, u32[]{:S(2)}) collective-permute-start(bf16[768,384]{1,0:T(8,128)(2,1)S(1)} %collective-permute-done.10.refs_3_), channel_id=1, source_target_pairs={{4,0},{6,2},{0,4},{2,6},{12,8},{14,10},{8,12},{10,14},{20,16},{22,... | collective-permute-start | bytes 1769480 | tf_op jit(solution)/shard_map/ppermute | solution.py:349
  27.1 0.0 collective-permute-done.15.refs_4_
  27.1 0.0 copy-done.4
  27.1 0.0 copy-done.6
  27.1 5.5 %attend.19 = (f32[392,384]{1,0:T(8,128)S(1)}, f32[392,384]{1,0:T(8,128)S(1)}) custom-call(s32[8,384]{1,0:T(8,128)S(1)} %get-tuple-element.98.bounds_ref, bf16[384,384]{1,0:T(8,128)(2,1)S(1)} %copy-done.4, bf16[384,384]{1,0:T(8,128)(2,1)S(1)} %copy-done.6, bf16[768,384]{1,0:T(8,128)(2,1)S(1)} %collective-permute-done.12.refs_2_, ...), custom_call_target="tpu_custom_call" | custom-call | flops 8153726976 | bytes 2949120 | tf_op jit(solution)/shard_map/attend/pallas_call | solution.py:235
  32.6 0.8 %collective-permute-done.13 = bf16[768,384]{1,0:T(8,128)(2,1)S(1)} collective-permute-done((bf16[768,384]{1,0:T(8,128)(2,1)S(1)}, bf16[768,384]{1,0:T(8,128)(2,1)S(1)}, u32[]{:S(2)}, u32[]{:S(2)}) %collective-permute-start.13) | collective-permute-done | bytes 589856 | tf_op jit(solution)/shard_map/ppermute | solution.py:349
  33.4 3.5 %collective-permute-done.11 = bf16[768,384]{1,0:T(8,128)(2,1)S(1)} collective-permute-done((bf16[768,384]{1,0:T(8,128)(2,1)S(1)}, bf16[768,384]{1,0:T(8,128)(2,1)S(1)}, u32[]{:S(2)}, u32[]{:S(2)}) %collective-permute-start.11) | collective-permute-done | bytes 589856 | tf_op jit(solution)/shard_map/ppermute | solution.py:349
  36.9 10.1 %conditional.1 = (bf16[192,768]{1,0:T(8,128)(2,1)S(1)}) conditional(s32[]{:T(128)} %bitcast, (s32[8,384]{1,0:T(8,128)S(1)}, bf16[384,384]{1,0:T(8,128)(2,1)S(1)}, bf16[768,384]{1,0:T(8,128)(2,1)S(1)}, bf16[768,384]{1,0:T(8,128)(2,1)S(1)}, f32[392,384]{1,0:T(8,128)S(1)}, /*index=5*/bf16[384,384]{1,0:T(8,128)(2,1)S(1)}, ...), branch_computations={%region_0.1_spmd, %region_1.2_spmd, %region_2.3_spmd} | conditional | flops 13589544960 | bytes 16367824 | solution.py:404
  36.9 1.5 %attend.11 = f32[392,384]{1,0:T(8,128)S(1)} custom-call(s32[8,384]{1,0:T(8,128)S(1)} %get-tuple-element.56.bounds_ref, bf16[384,384]{1,0:T(8,128)(2,1)S(1)} %get-tuple-element.62.refs_0_, bf16[768,384]{1,0:T(8,128)(2,1)S(1)} %get-tuple-element.59.refs_1_, bf16[768,384]{1,0:T(8,128)(2,1)S(1)} %get-tuple-element.60.refs_2_, ...), custom_call_target="tpu_custom_call" | custom-call | flops 2717908992 | bytes 1769472 | tf_op jit(solution)/shard_map/cond/branch_0_fun/attend/pallas_call | solution.py:235
  38.4 0.1 collective-permute-start
  38.5 1.5 %attend.10.refs_0_ = f32[392,384]{1,0:T(8,128)S(1)} custom-call(s32[8,384]{1,0:T(8,128)S(1)} %get-tuple-element.56.bounds_ref, bf16[384,384]{1,0:T(8,128)(2,1)S(1)} %get-tuple-element.58.refs_0_, bf16[768,384]{1,0:T(8,128)(2,1)S(1)} %get-tuple-element.59.refs_1_, bf16[768,384]{1,0:T(8,128)(2,1)S(1)} %get-tuple-element.60.refs_2_, ...), custom_call_target="tpu_custom_call" | custom-call | flops 2717908992 | bytes 1769472 | tf_op jit(solution)/shard_map/cond/branch_0_fun/attend/pallas_call | solution.py:235
  40.0 0.5 %collective-permute-done.refs_1_ = f32[392,384]{1,0:T(8,128)S(1)} collective-permute-done((f32[392,384]{1,0:T(8,128)S(1)}, f32[392,384]{1,0:T(8,128)S(1)}, u32[]{:S(2)}, u32[]{:S(2)}) %collective-permute-start) | collective-permute-done | bytes 602144 | tf_op jit(solution)/shard_map/cond/branch_0_fun/ppermute | solution.py:349
  40.5 0.3 part.3
  40.8 1.6 %collective-permute-start.1 = (bf16[192,384]{1,0:T(8,128)(2,1)S(1)}, bf16[192,384]{1,0:T(8,128)(2,1)S(1)}, u32[]{:S(2)}, u32[]{:S(2)}) collective-permute-start(bf16[192,384]{1,0:T(8,128)(2,1)S(1)} %get-tuple-element.65), channel_id=1, source_target_pairs={{0,1},{1,0},{2,3},{3,2},{4,5},{5,4},{6,7},{7,6},{8,9},{9,8},{10,11... | collective-permute-start | bytes 442376 | tf_op jit(solution)/shard_map/cond/branch_0_fun/ppermute | solution.py:312
  42.3 4.4 %collective-permute-done.1.got_ref = bf16[192,384]{1,0:T(8,128)(2,1)S(1)} collective-permute-done((bf16[192,384]{1,0:T(8,128)(2,1)S(1)}, bf16[192,384]{1,0:T(8,128)(2,1)S(1)}, u32[]{:S(2)}, u32[]{:S(2)}) %collective-permute-start.1) | collective-permute-done | bytes 147488 | tf_op jit(solution)/shard_map/cond/branch_0_fun/ppermute | solution.py:312
  47.0 0.0 copy-start.2
  47.0 0.7 %copy-done.2 = bf16[192,768]{1,0:T(8,128)(2,1)} copy-done((bf16[192,768]{1,0:T(8,128)(2,1)}, bf16[192,768]{1,0:T(8,128)(2,1)S(1)}, u32[]{:S(2)}) %copy-start.2) | copy-done | bytes 294936
  (1 shorter events, 0.0 us)
Async XLA Ops:
  0.0 11.0 %copy-start.3 = (bf16[384,384]{1,0:T(8,128)(2,1)S(1)}, bf16[384,384]{1,0:T(8,128)(2,1)}, u32[]{:S(2)}) copy-start(bf16[384,384]{1,0:T(8,128)(2,1)} %refs_0_.3) | copy-start | bytes 884740
  0.0 11.1 %copy-start.1 = (s32[5]{0:T(128)S(1)}, s32[5]{0:T(128)}, u32[]{:S(2)}) copy-start(s32[5]{0:T(128)} %tiles_ref.1) | copy-start | bytes 64
  2.1 11.5 %copy-start = (bf16[768,384]{1,0:T(8,128)(2,1)S(1)}, bf16[768,384]{1,0:T(8,128)(2,1)}, u32[]{:S(2)}) copy-start(bf16[768,384]{1,0:T(8,128)(2,1)} %pack.1.refs_2_) | copy-start | bytes 1769476
  2.1 16.6 %collective-permute-start.12 = (bf16[768,384]{1,0:T(8,128)(2,1)}, bf16[768,384]{1,0:T(8,128)(2,1)S(1)}, u32[]{:S(2)}, u32[]{:S(2)}) collective-permute-start(bf16[768,384]{1,0:T(8,128)(2,1)} %pack.1.refs_2_), channel_id=1, source_target_pairs={{4,0},{6,2},{0,4},{2,6},{12,8},{14,10},{8,12},{10,14},{20,16},{22,... | collective-permute-start | bytes 1769480 | tf_op jit(solution)/shard_map/ppermute | solution.py:349
  5.1 16.4 %collective-permute-start.10 = (bf16[768,384]{1,0:T(8,128)(2,1)}, bf16[768,384]{1,0:T(8,128)(2,1)S(1)}, u32[]{:S(2)}, u32[]{:S(2)}) collective-permute-start(bf16[768,384]{1,0:T(8,128)(2,1)} %pack.1.refs_2_), channel_id=1, source_target_pairs={{8,0},{14,6},{16,8},{2,10},{4,12},{22,14},{24,16},{10,18},{12,20},... | collective-permute-start | bytes 1769480 | tf_op jit(solution)/shard_map/ppermute | solution.py:349
  6.4 20.6 %collective-permute-start.15 = (bf16[768,384]{1,0:T(8,128)(2,1)}, bf16[768,384]{1,0:T(8,128)(2,1)S(1)}, u32[]{:S(2)}, u32[]{:S(2)}) collective-permute-start(bf16[768,384]{1,0:T(8,128)(2,1)} %pack.1.refs_2_), channel_id=1, source_target_pairs={{10,2},{12,4},{0,8},{18,10},{20,12},{6,14},{8,16},{26,18},{28,20},... | collective-permute-start | bytes 1769480 | tf_op jit(solution)/shard_map/ppermute | solution.py:349
  11.0 2.6 %collective-permute-start.14 = (bf16[384,384]{1,0:T(8,128)(2,1)S(1)}, bf16[384,384]{1,0:T(8,128)(2,1)S(1)}, u32[]{:S(2)}, u32[]{:S(2)}) collective-permute-start(bf16[384,384]{1,0:T(8,128)(2,1)S(1)} %copy-done.3), channel_id=1, source_target_pairs={{2,0},{0,2},{6,4},{4,6},{10,8},{8,10},{14,12},{12,14},{18,16},{16,... | collective-permute-start | bytes 884744 | tf_op jit(solution)/shard_map/ppermute | solution.py:349
  13.6 2.8 %copy-start.5 = (bf16[384,384]{1,0:T(8,128)(2,1)}, bf16[384,384]{1,0:T(8,128)(2,1)S(1)}, u32[]{:S(2)}) copy-start(bf16[384,384]{1,0:T(8,128)(2,1)S(1)} %collective-permute-done.14.refs_1_) | copy-start | bytes 884740
  16.4 10.6 %copy-start.4 = (bf16[384,384]{1,0:T(8,128)(2,1)S(1)}, bf16[384,384]{1,0:T(8,128)(2,1)}, u32[]{:S(2)}) copy-start(bf16[384,384]{1,0:T(8,128)(2,1)} %refs_0_.3) | copy-start | bytes 884740
  18.7 8.4 %copy-start.6 = (bf16[384,384]{1,0:T(8,128)(2,1)S(1)}, bf16[384,384]{1,0:T(8,128)(2,1)}, u32[]{:S(2)}) copy-start(bf16[384,384]{1,0:T(8,128)(2,1)} %copy-done.5) | copy-start | bytes 884740
  21.6 11.8 %collective-permute-start.13 = (bf16[768,384]{1,0:T(8,128)(2,1)S(1)}, bf16[768,384]{1,0:T(8,128)(2,1)S(1)}, u32[]{:S(2)}, u32[]{:S(2)}) collective-permute-start(bf16[768,384]{1,0:T(8,128)(2,1)S(1)} %broadcast_select_fusion), channel_id=1, source_target_pairs={{8,0},{14,6},{16,8},{2,10},{4,12},{22,14},{24,16},{10,18},{12,20},... | collective-permute-start | bytes 1769480 | tf_op jit(solution)/shard_map/ppermute | solution.py:349
  22.9 14.0 %collective-permute-start.11 = (bf16[768,384]{1,0:T(8,128)(2,1)S(1)}, bf16[768,384]{1,0:T(8,128)(2,1)S(1)}, u32[]{:S(2)}, u32[]{:S(2)}) collective-permute-start(bf16[768,384]{1,0:T(8,128)(2,1)S(1)} %collective-permute-done.10.refs_3_), channel_id=1, source_target_pairs={{4,0},{6,2},{0,4},{2,6},{12,8},{14,10},{8,12},{10,14},{20,16},{22,... | collective-permute-start | bytes 1769480 | tf_op jit(solution)/shard_map/ppermute | solution.py:349
  38.4 2.1 %collective-permute-start = (f32[392,384]{1,0:T(8,128)S(1)}, f32[392,384]{1,0:T(8,128)S(1)}, u32[]{:S(2)}, u32[]{:S(2)}) collective-permute-start(f32[392,384]{1,0:T(8,128)S(1)} %attend.11), channel_id=1, source_target_pairs={{2,0},{0,2},{6,4},{4,6},{10,8},{8,10},{14,12},{12,14},{18,16},{16,... | collective-permute-start | bytes 1806344 | tf_op jit(solution)/shard_map/cond/branch_0_fun/ppermute | solution.py:349
  40.8 6.0 %collective-permute-start.1 = (bf16[192,384]{1,0:T(8,128)(2,1)S(1)}, bf16[192,384]{1,0:T(8,128)(2,1)S(1)}, u32[]{:S(2)}, u32[]{:S(2)}) collective-permute-start(bf16[192,384]{1,0:T(8,128)(2,1)S(1)} %get-tuple-element.65), channel_id=1, source_target_pairs={{0,1},{1,0},{2,3},{3,2},{4,5},{5,4},{6,7},{7,6},{8,9},{9,8},{10,11... | collective-permute-start | bytes 442376 | tf_op jit(solution)/shard_map/cond/branch_0_fun/ppermute | solution.py:312
  47.0 0.7 %copy-start.2 = (bf16[192,768]{1,0:T(8,128)(2,1)}, bf16[192,768]{1,0:T(8,128)(2,1)S(1)}, u32[]{:S(2)}) copy-start(bf16[192,768]{1,0:T(8,128)(2,1)S(1)} %get-tuple-element.133) | copy-start | bytes 884740
where the time goes:
time: 47.6 us; the launch traced here: 47.7 us
  starting transfers between devices  16 us (34%)
  Pallas kernels  14.9 us (31%)
  waiting for transfers between devices  14.3 us (30%)
  between operations  1.47 us (3%)
  local copies, waits for them, and re-layouts  0.73 us (2%)
    ppermute x7, starting transfers between devices, moved(): return lax.ppermute(array, 'seq', pairs)  14.5 us
    pallas_call x4, Pallas kernels, attend(): pl.pallas_call(functools.partial(attend_kernel, which, places, arrays, no...  11.3 us
    ppermute x7, waiting for transfers between devices, moved(): return lax.ppermute(array, 'seq', pairs)  9.91 us
    ppermute x1, waiting for transfers between devices, finish_in_two(): got = lax.ppermute(send, 'head', [(0, 1), (1, 0)])  4.4 us
    pallas_call x1, Pallas kernels, pack(): pl.pallas_call(pack_kernel, out_shape=jax.ShapeDtypeStruct((2 * rows, col...  2.08 us
    ppermute x1, starting transfers between devices, finish_in_two(): got = lax.ppermute(send, 'head', [(0, 1), (1, 0)])  1.56 us
    pallas_call x1, Pallas kernels, meta(): pl.pallas_call(functools.partial(meta_kernel, halves), out_shape=[jax.Sha...  1.19 us
  transfers between devices with their start and end apart: 8, of which 6 were waited for; matrix products, arithmetic and copies ran while one was open for 0% of the time, Pallas kernels for 23%

commit v1 on v0

--- a/solution.py
+++ b/solution.py
@@ -22,7 +22,7 @@
 
 
 def params():
-    return pltpu.CompilerParams(vmem_limit_bytes=32 * 1024 * 1024)
+    return pltpu.CompilerParams(vmem_limit_bytes=16 * 1024 * 1024)
 
 
 def head_columns(h):
@@ -366,14 +366,19 @@
     has_corner = lambda s: (core(s) == 1) | ((s // 2) % 2 == 1)
     CORNER = lambda s: jnp.where(has_corner(s), s + 8 * (1 - 2 * core(s)), nobody) * tiles
 
+    def over_y(array):
+        both = lax.all_gather(array, "seq", axis_index_groups=pairs)
+        return lax.dynamic_index_in_dim(both, 1 - (lax.axis_index("seq") // 2) % 2, 0, keepdims=False)
+
+    pairs = [[s, s + 2] for s in range(owner_count) if (s // 2) % 2 == 0]
     block = pack(keys, values)
-    y1, a1, b1 = moved(block, across), moved(block, along), moved(block, against)
+    y1, a1, b1 = over_y(block), moved(block, along), moved(block, against)
     bounds, spans = meta(lambda s: [s, sibling(s)], image_tiles, rows)
     both = (queries, moved(queries, sibling))
     fold = functools.partial(attend, bounds, both)
     states = fold([block], [OWN], [])
+    ya = over_y(a1)
     ay = moved(jnp.where((spans == 0) | (core(lax.axis_index("seq")) == 1), y1, a1), along)
-    ya = moved(a1, across)
     states = fold([y1, a1, b1], [Y1, A1, B1], states)
 
     def last(blocks, places, states, shifts=None):

time: 47.6 us -> 93.3 us (1.96); the launches traced: 47.7 us -> 91.4 us
  waiting for transfers between devices: 14.3 us -> 40.3 us
  between operations: 1.47 us -> 14.9 us
  local copies, waits for them, and re-layouts: 0.73 us -> 3.39 us
  Pallas kernels: 14.9 us -> 12.6 us
  other arithmetic: 0.07 us -> 2.04 us
  starting transfers between devices: 16 us -> 17.8 us
    all_gather x0 -> x2, waiting for transfers between devices: none -> 21.7 us  [over_y(): both = lax.all_gather(array, 'seq', axis_index_groups=pairs)]
    ppermute x7 -> x8, waiting for transfers between devices: 9.91 us -> 13.9 us  [moved(): return lax.ppermute(array, 'seq', pairs)]
    pallas_call x4 -> x5, Pallas kernels: 11.3 us -> 8.96 us  [attend(): pl.pallas_call(functools.partial(attend_kernel, which, places, arrays, no...]
    select_n x1, other arithmetic: 0.07 us -> 2.04 us  [paired_shards(): jnp.where((spans == 0) | (core(lax.axis_index('seq')) == 1), y1, a1)]
    ppermute x7 -> x8, starting transfers between devices: 14.5 us -> 16.3 us  [moved(): return lax.ppermute(array, 'seq', pairs)]
    unnamed x14 -> x22, local copies, waits for them, and re-layouts: 0.73 us -> 2.26 us
    squeeze x0 -> x1, local copies, waits for them, and re-layouts: none -> 1.12 us  [over_y(): lax.dynamic_index_in_dim(both, 1 - lax.axis_index('seq') // 2 % 2, 0, kee...]
  transfers between devices with their start and end apart: 8 -> 11, of which waited for: 6 -> 7; matrix products, arithmetic and copies ran while one was open for 0% -> 3% of each run, Pallas kernels for 23% -> 11%
where the time goes in v1:
time: 93.3 us; the launch traced here: 91.4 us
  waiting for transfers between devices  40.3 us (43%)
  starting transfers between devices  17.8 us (19%)
  between operations  14.9 us (16%)
  Pallas kernels  12.6 us (14%)
  local copies, waits for them, and re-layouts  3.39 us (4%)
  other arithmetic  2.04 us (2%)
    all_gather x2, waiting for transfers between devices, over_y(): both = lax.all_gather(array, 'seq', axis_index_groups=pairs)  21.7 us
    ppermute x8, starting transfers between devices, moved(): return lax.ppermute(array, 'seq', pairs)  16.3 us
    ppermute x8, waiting for transfers between devices, moved(): return lax.ppermute(array, 'seq', pairs)  13.9 us
    pallas_call x5, Pallas kernels, attend(): pl.pallas_call(functools.partial(attend_kernel, which, places, arrays, no...  8.96 us
    ppermute x1, waiting for transfers between devices, finish_in_two(): got = lax.ppermute(send, 'head', [(0, 1), (1, 0)])  4.65 us
    unnamed x22, local copies, waits for them, and re-layouts  2.26 us
    pallas_call x1, Pallas kernels, pack(): pl.pallas_call(pack_kernel, out_shape=jax.ShapeDtypeStruct((2 * rows, col...  2.08 us
    select_n x1, other arithmetic, paired_shards(): jnp.where((spans == 0) | (core(lax.axis_index('seq')) == 1), y1, a1)  2.04 us
  transfers between devices with their start and end apart: 11, of which 7 were waited for; matrix products, arithmetic and copies ran while one was open for 3% of the time, Pallas kernels for 11%

profile of v1, /device:TPU:0, one launch (start us, length us, event | category | flops | bytes accessed | tf_op | source)
XLA Modules:
  0.0 91.4 jit_solution(9157312989847349510)
XLA Ops:
  6.5 0.0 all-gather.7.cloned.1.call-start
  6.5 2.1 %pack.1.refs_2_ = bf16[768,384]{1,0:T(8,128)(2,1)} custom-call(bf16[384,384]{1,0:T(8,128)(2,1)} %k_ref.1, bf16[384,384]{1,0:T(8,128)(2,1)} %v_ref.1), custom_call_target="tpu_custom_call" | custom-call | tf_op jit(solution)/shard_map/pack/pallas_call | solution.py:106
  8.6 0.0 all-gather.7.cloned.1.call-update
  8.7 0.0 copy-start
  8.7 0.0 all-gather.5.cloned.1.call-start
  8.7 1.4 %collective-permute-start.10 = (bf16[768,384]{1,0:T(8,128)(2,1)}, bf16[768,384]{1,0:T(8,128)(2,1)S(1)}, u32[]{:S(2)}, u32[]{:S(2)}) collective-permute-start(bf16[768,384]{1,0:T(8,128)(2,1)} %pack.1.refs_2_), channel_id=1, source_target_pairs={{8,0},{14,6},{16,8},{2,10},{4,12},{22,14},{24,16},{10,18},{12,20},... | collective-permute-start | bytes 1769480 | tf_op jit(solution)/shard_map/ppermute | solution.py:349
  10.1 5.6 %collective-permute-start.13 = (bf16[768,384]{1,0:T(8,128)(2,1)}, bf16[768,384]{1,0:T(8,128)(2,1)S(1)}, u32[]{:S(2)}, u32[]{:S(2)}) collective-permute-start(bf16[768,384]{1,0:T(8,128)(2,1)} %pack.1.refs_2_), channel_id=1, source_target_pairs={{10,2},{12,4},{0,8},{18,10},{20,12},{6,14},{8,16},{26,18},{28,20},... | collective-permute-start | bytes 1769480 | tf_op jit(solution)/shard_map/ppermute | solution.py:349
  15.7 0.0 copy-done.7
  15.8 0.1 collective-permute-start.12
  15.8 0.0 copy-done.1
  15.8 1.2 %meta.1 = (s32[8,384]{1,0:T(8,128)S(1)}, s32[1]{0:T(128)}) custom-call(s32[5]{0:T(128)S(1)} %copy-done.1), custom_call_target="tpu_custom_call" | custom-call | flops 3221225472 | tf_op jit(solution)/shard_map/meta/pallas_call | solution.py:75
  18.4 7.2 %collective-permute-done.10.refs_3_ = bf16[768,384]{1,0:T(8,128)(2,1)S(1)} collective-permute-done((bf16[768,384]{1,0:T(8,128)(2,1)}, bf16[768,384]{1,0:T(8,128)(2,1)S(1)}, u32[]{:S(2)}, u32[]{:S(2)}) %collective-permute-start.10) | collective-permute-done | bytes 589856 | tf_op jit(solution)/shard_map/ppermute | solution.py:349
  25.5 0.8 copy-done.2
  26.4 0.0 all-gather.5.cloned.1.call-update
  26.4 0.0 collective-permute-done.12.refs_1_
  26.4 0.0 copy-start.8
  26.4 0.7 copy-done.8
  27.1 3.8 %attend.18 = (f32[392,384]{1,0:T(8,128)S(1)}, f32[392,384]{1,0:T(8,128)S(1)}) custom-call(s32[8,384]{1,0:T(8,128)S(1)} %get-tuple-element.98.bounds_ref, bf16[384,384]{1,0:T(8,128)(2,1)S(1)} %copy-done.7, bf16[384,384]{1,0:T(8,128)(2,1)} %copy-done.8, bf16[768,384]{1,0:T(8,128)(2,1)S(1)} %copy-done), custom_call_target="tpu_custom_call" | custom-call | flops 2717908992 | bytes 1769472 | tf_op jit(solution)/shard_map/attend/pallas_call | solution.py:235
  30.9 3.5 %all-gather.7.cloned.1.call-done = bf16[1536,384]{1,0:T(8,128)(2,1)} async-done(((bf16[768,384]{1,0:T(8,128)(2,1)}), bf16[1536,384]{1,0:T(8,128)(2,1)}) %all-gather.7.cloned.1.call-update) | async-done | bytes 1179664 | tf_op jit(solution)/shard_map/all_gather | solution.py:370
  34.4 2.0 %broadcast_select_fusion = (bf16[768,384]{1,0:T(8,128)(2,1)}, bf16[768,384]{1,0:T(8,128)(2,1)S(1)}) fusion(bf16[768,384]{1,0:T(8,128)(2,1)S(1)} %copy-done.3, pred[]{:T(512)S(6)} %or.3, bf16[2,768,384]{2,1,0:T(8,128)(2,1)} %bitcast.10, s32[]{:T(128)S(6)} %select_n.33), kind=kLoop, calls=%fused_computation.2 | loop fusion | flops 294912 | bytes 2359301 | tf_op jit(solution)/shard_map/jit(_where)/select_n | solution.py:381
  36.5 1.3 %collective-permute-start.11 = (bf16[768,384]{1,0:T(8,128)(2,1)}, bf16[768,384]{1,0:T(8,128)(2,1)}, u32[]{:S(2)}, u32[]{:S(2)}) collective-permute-start(bf16[768,384]{1,0:T(8,128)(2,1)} %get-tuple-element.104), channel_id=1, source_target_pairs={{8,0},{14,6},{16,8},{2,10},{4,12},{22,14},{24,16},{10,18},{12,20},... | collective-permute-start | bytes 1769480 | tf_op jit(solution)/shard_map/ppermute | solution.py:349
  37.8 0.0 collective-permute-done.13.refs_4_
  37.8 2.8 %attend.19 = (f32[392,384]{1,0:T(8,128)}, f32[392,384]{1,0:T(8,128)}) custom-call(s32[8,384]{1,0:T(8,128)S(1)} %get-tuple-element.98.bounds_ref, bf16[384,384]{1,0:T(8,128)(2,1)S(1)} %copy-done.7, bf16[384,384]{1,0:T(8,128)(2,1)S(1)} %copy-done.9, bf16[768,384]{1,0:T(8,128)(2,1)S(1)} %get-tuple-element.105.refs_2_, bf16[768,384]{1,0:T(8,128)(2,1)S(1)} %copy-done.3, ...), custom_call_target="tpu_custom_call" | custom-call | flops 8153726976 | bytes 2949120 | tf_op jit(solution)/shard_map/attend/pallas_call | solution.py:235
  40.6 18.2 %all-gather.5.cloned.1.call-done = bf16[1536,384]{1,0:T(8,128)(2,1)} async-done(((bf16[768,384]{1,0:T(8,128)(2,1)}), bf16[1536,384]{1,0:T(8,128)(2,1)}) %all-gather.5.cloned.1.call-update) | async-done | bytes 1179664 | tf_op jit(solution)/shard_map/all_gather | solution.py:370
  58.8 1.1 %dynamic-slice_bitcast_fusion.1 = bf16[768,384]{1,0:T(8,128)(2,1)S(1)} fusion(bf16[2,768,384]{2,1,0:T(8,128)(2,1)} %bitcast.9, s32[]{:T(128)S(6)} %select_n.33), kind=kLoop, calls=%fused_computation.1 | loop fusion | bytes 1179652 | tf_op jit(solution)/shard_map/jit(dynamic_index_in_dim)/squeeze | solution.py:371
  59.9 0.0 collective-permute-done.11
  59.9 23.9 %conditional.1 = (bf16[192,768]{1,0:T(8,128)(2,1)S(1)}) conditional(s32[]{:T(128)} %bitcast, (s32[8,384]{1,0:T(8,128)S(1)}, bf16[384,384]{1,0:T(8,128)(2,1)S(1)}, bf16[768,384]{1,0:T(8,128)(2,1)S(1)}, bf16[768,384]{1,0:T(8,128)(2,1)}, f32[392,384]{1,0:T(8,128)}, /*index=5*/bf16[384,384]{1,0:T(8,128)(2,1)S(1)}, ...), branch_computations={%region_0.1_spmd, %region_1.2_spmd, %region_2.3_spmd} | conditional | flops 13589544960 | bytes 21184776 | solution.py:409
  60.0 0.0 copy-start.12
  60.0 0.0 copy-start.13
  60.0 1.4 %collective-permute-start.6 = (bf16[768,384]{1,0:T(8,128)(2,1)S(1)}, bf16[768,384]{1,0:T(8,128)(2,1)S(1)}, u32[]{:S(2)}, u32[]{:S(2)}) collective-permute-start(bf16[768,384]{1,0:T(8,128)(2,1)S(1)} %get-tuple-element.80), channel_id=1, source_target_pairs={{8,0},{16,8},{4,12},{24,16},{12,20},{20,28},{9,1},{17,9},{5,13},{2... | collective-permute-start | bytes 1769480 | tf_op jit(solution)/shard_map/cond/branch_2_fun/ppermute | solution.py:349
  61.4 4.6 %collective-permute-start.5 = (bf16[768,384]{1,0:T(8,128)(2,1)}, bf16[768,384]{1,0:T(8,128)(2,1)S(1)}, u32[]{:S(2)}, u32[]{:S(2)}) collective-permute-start(bf16[768,384]{1,0:T(8,128)(2,1)} %get-tuple-element.79.refs_3_), channel_id=1, source_target_pairs={{4,0},{0,4},{14,6},{12,8},{2,10},{8,12},{22,14},{20,16},{10,18},{1... | collective-permute-start | bytes 1769480 | tf_op jit(solution)/shard_map/cond/branch_2_fun/ppermute | solution.py:349
  66.0 0.1 corner.1
  66.1 0.9 collective-permute-start.7
  67.0 0.0 copy-done.12
  67.0 0.0 copy-done.13
  67.0 1.5 %attend.15 = (f32[392,384]{1,0:T(8,128)S(1)}, f32[392,384]{1,0:T(8,128)S(1)}) custom-call(s32[8,384]{1,0:T(8,128)S(1)} %get-tuple-element.77.bounds_ref, bf16[384,384]{1,0:T(8,128)(2,1)S(1)} %get-tuple-element.78.refs_0_, bf16[384,384]{1,0:T(8,128)(2,1)S(1)} %get-tuple-element.83.refs_1_.refs_0_, bf16[768,384]{1,0:T(8,128)(2,1)S(1)} %get-tuple-element.84.refs_2_, ...), custom_call_target="tpu_custom_call" | custom-call | flops 5435817984 | bytes 2359296 | tf_op jit(solution)/shard_map/cond/branch_2_fun/attend/pallas_call | solution.py:235
  68.5 0.0 collective-permute-done.7.refs_3_
  68.5 3.4 %collective-permute-done.6.refs_2_ = bf16[768,384]{1,0:T(8,128)(2,1)S(1)} collective-permute-done((bf16[768,384]{1,0:T(8,128)(2,1)S(1)}, bf16[768,384]{1,0:T(8,128)(2,1)S(1)}, u32[]{:S(2)}, u32[]{:S(2)}) %collective-permute-start.6) | collective-permute-done | bytes 589856 | tf_op jit(solution)/shard_map/cond/branch_2_fun/ppermute | solution.py:349
  71.9 2.2 %collective-permute-done.5.refs_1_ = bf16[768,384]{1,0:T(8,128)(2,1)S(1)} collective-permute-done((bf16[768,384]{1,0:T(8,128)(2,1)}, bf16[768,384]{1,0:T(8,128)(2,1)S(1)}, u32[]{:S(2)}, u32[]{:S(2)}) %collective-permute-start.5) | collective-permute-done | bytes 589856 | tf_op jit(solution)/shard_map/cond/branch_2_fun/ppermute | solution.py:349
  74.1 0.4 attend.17
  74.5 1.0 %collective-permute-start.8 = (f32[392,384]{1,0:T(8,128)S(1)}, f32[392,384]{1,0:T(8,128)S(1)}, u32[]{:S(2)}, u32[]{:S(2)}) collective-permute-start(f32[392,384]{1,0:T(8,128)S(1)} %attend.17), channel_id=1, source_target_pairs={{2,0},{0,2},{6,4},{4,6},{10,8},{8,10},{14,12},{12,14},{18,16},{16,... | collective-permute-start | bytes 1806344 | tf_op jit(solution)/shard_map/cond/branch_2_fun/ppermute | solution.py:349
  75.5 0.4 attend.16.refs_0_
  75.9 1.2 %collective-permute-done.8.refs_1_ = f32[392,384]{1,0:T(8,128)S(1)} collective-permute-done((f32[392,384]{1,0:T(8,128)S(1)}, f32[392,384]{1,0:T(8,128)S(1)}, u32[]{:S(2)}, u32[]{:S(2)}) %collective-permute-start.8) | collective-permute-done | bytes 602144 | tf_op jit(solution)/shard_map/cond/branch_2_fun/ppermute | solution.py:349
  77.2 0.3 part.5
  77.4 1.5 %collective-permute-start.9 = (bf16[192,384]{1,0:T(8,128)(2,1)S(1)}, bf16[192,384]{1,0:T(8,128)(2,1)S(1)}, u32[]{:S(2)}, u32[]{:S(2)}) collective-permute-start(bf16[192,384]{1,0:T(8,128)(2,1)S(1)} %get-tuple-element.90), channel_id=1, source_target_pairs={{0,1},{1,0},{2,3},{3,2},{4,5},{5,4},{6,7},{7,6},{8,9},{9,8},{10,11... | collective-permute-start | bytes 442376 | tf_op jit(solution)/shard_map/cond/branch_2_fun/ppermute | solution.py:312
  79.0 4.6 %collective-permute-done.9.got_ref = bf16[192,384]{1,0:T(8,128)(2,1)S(1)} collective-permute-done((bf16[192,384]{1,0:T(8,128)(2,1)S(1)}, bf16[192,384]{1,0:T(8,128)(2,1)S(1)}, u32[]{:S(2)}, u32[]{:S(2)}) %collective-permute-start.9) | collective-permute-done | bytes 147488 | tf_op jit(solution)/shard_map/cond/branch_2_fun/ppermute | solution.py:312
  83.9 0.0 copy-start.6
  83.9 0.7 copy-done.6
  (15 shorter events, 0.1 us)
Async XLA Ops:
  6.5 9.2 %copy-start.7 = (bf16[384,384]{1,0:T(8,128)(2,1)S(1)}, bf16[384,384]{1,0:T(8,128)(2,1)}, u32[]{:S(2)}) copy-start(bf16[384,384]{1,0:T(8,128)(2,1)} %refs_0_.3) | copy-start | bytes 884740
  6.5 9.3 %copy-start.1 = (s32[5]{0:T(128)S(1)}, s32[5]{0:T(128)}, u32[]{:S(2)}) copy-start(s32[5]{0:T(128)} %tiles_ref.1) | copy-start | bytes 64
  6.5 27.9 %all-gather.7.cloned.1.call-start = ((), (), s32[]{:S(2)}) async-start(), calls=%async_computation.1 | async-start | bytes 1769472 | tf_op jit(solution)/shard_map/all_gather | solution.py:370
  8.7 18.5 %copy-start = (bf16[768,384]{1,0:T(8,128)(2,1)S(1)}, bf16[768,384]{1,0:T(8,128)(2,1)}, u32[]{:S(2)}) copy-start(bf16[768,384]{1,0:T(8,128)(2,1)} %pack.1.refs_2_) | copy-start | bytes 1769476
  8.7 50.1 %all-gather.5.cloned.1.call-start = ((), (), s32[]{:S(2)}) async-start(), calls=%async_computation | async-start | bytes 1769472 | tf_op jit(solution)/shard_map/all_gather | solution.py:370
  8.7 16.8 %collective-permute-start.10 = (bf16[768,384]{1,0:T(8,128)(2,1)}, bf16[768,384]{1,0:T(8,128)(2,1)S(1)}, u32[]{:S(2)}, u32[]{:S(2)}) collective-permute-start(bf16[768,384]{1,0:T(8,128)(2,1)} %pack.1.refs_2_), channel_id=1, source_target_pairs={{8,0},{14,6},{16,8},{2,10},{4,12},{22,14},{24,16},{10,18},{12,20},... | collective-permute-start | bytes 1769480 | tf_op jit(solution)/shard_map/ppermute | solution.py:349
  10.1 27.6 %collective-permute-start.13 = (bf16[768,384]{1,0:T(8,128)(2,1)}, bf16[768,384]{1,0:T(8,128)(2,1)S(1)}, u32[]{:S(2)}, u32[]{:S(2)}) collective-permute-start(bf16[768,384]{1,0:T(8,128)(2,1)} %pack.1.refs_2_), channel_id=1, source_target_pairs={{10,2},{12,4},{0,8},{18,10},{20,12},{6,14},{8,16},{26,18},{28,20},... | collective-permute-start | bytes 1769480 | tf_op jit(solution)/shard_map/ppermute | solution.py:349
  15.8 10.6 %collective-permute-start.12 = (bf16[384,384]{1,0:T(8,128)(2,1)S(1)}, bf16[384,384]{1,0:T(8,128)(2,1)S(1)}, u32[]{:S(2)}, u32[]{:S(2)}) collective-permute-start(bf16[384,384]{1,0:T(8,128)(2,1)S(1)} %copy-done.7), channel_id=1, source_target_pairs={{2,0},{0,2},{6,4},{4,6},{10,8},{8,10},{14,12},{12,14},{18,16},{16,... | collective-permute-start | bytes 884744 | tf_op jit(solution)/shard_map/ppermute | solution.py:349
  25.5 0.8 copy-start.2
  26.4 0.7 copy-start.8
  27.1 7.3 %copy-start.3 = (bf16[768,384]{1,0:T(8,128)(2,1)S(1)}, bf16[768,384]{1,0:T(8,128)(2,1)}, u32[]{:S(2)}) copy-start(bf16[768,384]{1,0:T(8,128)(2,1)} %copy-done.2) | copy-start | bytes 1769476
  34.4 3.4 %copy-start.9 = (bf16[384,384]{1,0:T(8,128)(2,1)S(1)}, bf16[384,384]{1,0:T(8,128)(2,1)}, u32[]{:S(2)}) copy-start(bf16[384,384]{1,0:T(8,128)(2,1)} %copy-done.8) | copy-start | bytes 884740
  36.5 1.3 %copy-start.4 = (bf16[768,384]{1,0:T(8,128)(2,1)}, bf16[768,384]{1,0:T(8,128)(2,1)S(1)}, u32[]{:S(2)}) copy-start(bf16[768,384]{1,0:T(8,128)(2,1)S(1)} %get-tuple-element.105.refs_2_) | copy-start | bytes 1769476
  36.5 23.4 %collective-permute-start.11 = (bf16[768,384]{1,0:T(8,128)(2,1)}, bf16[768,384]{1,0:T(8,128)(2,1)}, u32[]{:S(2)}, u32[]{:S(2)}) collective-permute-start(bf16[768,384]{1,0:T(8,128)(2,1)} %get-tuple-element.104), channel_id=1, source_target_pairs={{8,0},{14,6},{16,8},{2,10},{4,12},{22,14},{24,16},{10,18},{12,20},... | collective-permute-start | bytes 1769480 | tf_op jit(solution)/shard_map/ppermute | solution.py:349
  40.6 19.3 %copy-start.5 = (bf16[768,384]{1,0:T(8,128)(2,1)S(1)}, bf16[768,384]{1,0:T(8,128)(2,1)}, u32[]{:S(2)}) copy-start(bf16[768,384]{1,0:T(8,128)(2,1)} %copy-done.4) | copy-start | bytes 1769476
  40.6 19.3 %copy-start.10 = (bf16[384,384]{1,0:T(8,128)(2,1)S(1)}, bf16[384,384]{1,0:T(8,128)(2,1)}, u32[]{:S(2)}) copy-start(bf16[384,384]{1,0:T(8,128)(2,1)} %copy-done.8) | copy-start | bytes 884740
  60.0 7.0 %copy-start.12 = (f32[392,384]{1,0:T(8,128)S(1)}, f32[392,384]{1,0:T(8,128)}, u32[]{:S(2)}) copy-start(f32[392,384]{1,0:T(8,128)} %get-tuple-element.85.refs_4_) | copy-start | bytes 1806340 | tf_op jit(solution)/shard_map/cond
  60.0 7.0 %copy-start.13 = (f32[392,384]{1,0:T(8,128)S(1)}, f32[392,384]{1,0:T(8,128)}, u32[]{:S(2)}) copy-start(f32[392,384]{1,0:T(8,128)} %get-tuple-element.86.refs_5_) | copy-start | bytes 1806340 | tf_op jit(solution)/shard_map/cond
  60.0 11.9 %collective-permute-start.6 = (bf16[768,384]{1,0:T(8,128)(2,1)S(1)}, bf16[768,384]{1,0:T(8,128)(2,1)S(1)}, u32[]{:S(2)}, u32[]{:S(2)}) collective-permute-start(bf16[768,384]{1,0:T(8,128)(2,1)S(1)} %get-tuple-element.80), channel_id=1, source_target_pairs={{8,0},{16,8},{4,12},{24,16},{12,20},{20,28},{9,1},{17,9},{5,13},{2... | collective-permute-start | bytes 1769480 | tf_op jit(solution)/shard_map/cond/branch_2_fun/ppermute | solution.py:349
  61.4 12.7 %collective-permute-start.5 = (bf16[768,384]{1,0:T(8,128)(2,1)}, bf16[768,384]{1,0:T(8,128)(2,1)S(1)}, u32[]{:S(2)}, u32[]{:S(2)}) collective-permute-start(bf16[768,384]{1,0:T(8,128)(2,1)} %get-tuple-element.79.refs_3_), channel_id=1, source_target_pairs={{4,0},{0,4},{14,6},{12,8},{2,10},{8,12},{22,14},{20,16},{10,18},{1... | collective-permute-start | bytes 1769480 | tf_op jit(solution)/shard_map/cond/branch_2_fun/ppermute | solution.py:349
  66.1 2.4 %collective-permute-start.7 = (bf16[512,384]{1,0:T(8,128)(2,1)S(1)}, bf16[512,384]{1,0:T(8,128)(2,1)S(1)}, u32[]{:S(2)}, u32[]{:S(2)}) collective-permute-start(bf16[512,384]{1,0:T(8,128)(2,1)S(1)} %corner.1), channel_id=1, source_target_pairs={{12,4},{2,10},{20,12},{6,14},{10,18},{28,20},{14,22},{18,26},{22,3... | collective-permute-start | bytes 1179656 | tf_op jit(solution)/shard_map/cond/branch_2_fun/ppermute | solution.py:349
  74.5 2.7 %collective-permute-start.8 = (f32[392,384]{1,0:T(8,128)S(1)}, f32[392,384]{1,0:T(8,128)S(1)}, u32[]{:S(2)}, u32[]{:S(2)}) collective-permute-start(f32[392,384]{1,0:T(8,128)S(1)} %attend.17), channel_id=1, source_target_pairs={{2,0},{0,2},{6,4},{4,6},{10,8},{8,10},{14,12},{12,14},{18,16},{16,... | collective-permute-start | bytes 1806344 | tf_op jit(solution)/shard_map/cond/branch_2_fun/ppermute | solution.py:349
  77.4 6.2 %collective-permute-start.9 = (bf16[192,384]{1,0:T(8,128)(2,1)S(1)}, bf16[192,384]{1,0:T(8,128)(2,1)S(1)}, u32[]{:S(2)}, u32[]{:S(2)}) collective-permute-start(bf16[192,384]{1,0:T(8,128)(2,1)S(1)} %get-tuple-element.90), channel_id=1, source_target_pairs={{0,1},{1,0},{2,3},{3,2},{4,5},{5,4},{6,7},{7,6},{8,9},{9,8},{10,11... | collective-permute-start | bytes 442376 | tf_op jit(solution)/shard_map/cond/branch_2_fun/ppermute | solution.py:312
  83.9 0.7 copy-start.6
Sparse Core Ops, SparseCore 0:
  8.9 25.4 all-gather.6
  36.0 22.7 all-gather.4
